TPU v7x, 512 devices: a whole 4x4x16 slice. The times are simulated.
512 devices in a mesh: band: 128 (over y, z, core), chan: 4 (over x).
Axes of the slice: x: 4, y: 4, z: 16, core: 2. Of those that a mesh axis runs over, the one named last changes fastest.
Arguments:
- spectra: bfloat16 [2, 2, 16384, 1024], P(None, None, 'chan', 'band')
- window_flags: int32 [2, 128], replicated, may hold values 0 or 1
- pair_tiles: int32 [4, 128, 2], P('chan'), may hold values from 0 to 127, as said below
- owners: int32 [4, 128, 1], P('chan'), may hold values from 0 to 127; in each aligned block of 128 rows (0 to 127, 128 to 255, ..., all dimensions but the last counted through in order) at most 2 rows name the same one
- stacks: float32 [4, 256, 512, 128], P('chan', 'band'), may hold values from -3 to 3
Outputs:
- new_stacks: float32 [4, 256, 512, 128], P('chan', 'band')
Inputs may be any that keep to these rules, and one draw needn't show every extreme that they name: `pair_tiles`: entry 0 is a tile of the pair's own quarter q (q * 32 to q * 32 + 31) and entry 1 = entry 0 + d: either 0 <= d <= 7, with d even where entry 1 lies in the quarter above, or -7 <= d < 0 with entry 1 in the quarter below and d odd. No two pair tiles of the whole cable join the same two tiles. Every quarter has a pair with d = 7, and every quarter but the first one with d = -7. `owners`: no owner holds more than 2 pair tiles of one quarter; some owner holds exactly 2.
All inputs are finite; a program needn't handle non-finite values.
Results may differ from a plain program's by a relative error of at most 0.0039.
Values may be sent and summed in bfloat16 or wider, within the bound.
A program may use at most 64 MiB of HBM per device.

v0:
```python
import math

import jax
import jax.numpy as jnp
from jax import lax
from jax.sharding import PartitionSpec as P

TILE = 128
MAXOFF = 7
LAGS = 512
CAP = 2


STABILITY_FLOOR = 1e-05


def padded(shard, sides, width):
    for axis, dim in sides:
        size, length = (lax.axis_size(axis), shard.shape[dim])
        up = [(i, (i + 1) % size) for i in range(size - 1)]
        down = [(j, i) for i, j in up]
        last = lax.slice_in_dim(shard, length - width, length, axis=dim)
        first = lax.slice_in_dim(shard, 0, width, axis=dim)
        before = lax.ppermute(last, axis, up)
        after = lax.ppermute(first, axis, down)
        shard = jnp.concatenate([before, shard, after], axis=dim)
    return shard


def lag_table(first_bin, bin_count, total_bins):
    frequency = first_bin + lax.iota(jnp.int32, bin_count)
    lag_shift = lax.iota(jnp.int32, LAGS) - LAGS // 2
    phase_index = jnp.mod(lag_shift[:, None] * frequency[None, :], total_bins)
    angles = phase_index.astype(jnp.float32) * (2.0 * math.pi / total_bins)
    amplitude = 1.0 / math.sqrt(total_bins)
    return jnp.concatenate(
        [jnp.cos(angles) * amplitude, -jnp.sin(angles) * amplitude], axis=1
    ).astype(jnp.bfloat16)


def whiten(spectra, window_flags, quarter):
    tiles_here = spectra.shape[2] // TILE
    values = spectra.astype(jnp.float32)
    energy = values[:, 0] * values[:, 0] + values[:, 1] * values[:, 1]
    level = jnp.sqrt(jnp.mean(energy, axis=-1) + STABILITY_FLOOR)
    tile_validity_flags = lax.dynamic_slice_in_dim(
        window_flags, quarter * tiles_here, tiles_here, 1
    ).astype(jnp.float32)
    gate = jnp.repeat(tile_validity_flags, TILE, axis=1)
    return (values / level[:, None, :, None] * gate[:, None, :, None]).astype(jnp.bfloat16)


def block_cross(left_tiles, right_tiles, divisor):
    left_real = left_tiles[:, 0].astype(jnp.float32)
    left_imag = left_tiles[:, 1].astype(jnp.float32)
    right_real = right_tiles[:, 0].astype(jnp.float32)
    right_imag = right_tiles[:, 1].astype(jnp.float32)
    real_part = jnp.sum(left_real * right_real + left_imag * right_imag, axis=0)
    imaginary_component = jnp.sum(left_real * right_imag - left_imag * right_real, axis=0)
    return (
        jnp.concatenate([real_part, imaginary_component], axis=-1) / divisor[:, None, None]
    ).astype(jnp.bfloat16)


def body(spectra, window_flags, pair_tiles, owners, stacks):
    quarter = lax.axis_index("chan")
    band_size = lax.axis_size("band")
    bin_count = spectra.shape[3]
    tiles_here = spectra.shape[2] // TILE
    whitened = whiten(spectra, window_flags, quarter)
    extended = padded(whitened, (("chan", 2),), MAXOFF * TILE)
    offset = quarter * tiles_here - MAXOFF
    tile_blocks = extended.reshape(extended.shape[0], 2, extended.shape[2] // TILE, TILE, bin_count)
    pair_list = pair_tiles[0]
    owner_ids = owners[0, :, 0]
    count_pairs = pair_list.shape[0]
    source = pair_list[:, 0]
    target = pair_list[:, 1]
    flags_real = window_flags.astype(jnp.float32)
    columns = lax.iota(jnp.int32, window_flags.shape[1])
    pick_source = (source[:, None] == columns[None, :]).astype(jnp.float32)
    pick_target = (target[:, None] == columns[None, :]).astype(jnp.float32)
    source_flags = jnp.dot(pick_source, flags_real.T, precision=lax.Precision.HIGHEST)
    target_flags = jnp.dot(pick_target, flags_real.T, precision=lax.Precision.HIGHEST)
    divisor = jnp.maximum(jnp.sum(source_flags * target_flags, axis=1), 1.0)
    local_source = source - offset
    local_target = target - offset
    position = lax.iota(jnp.int32, count_pairs)
    earlier = (owner_ids[:, None] == owner_ids[None, :]) & (position[None, :] < position[:, None])
    slot_rank = jnp.sum(earlier.astype(jnp.int32), axis=1)
    slot_index = owner_ids * CAP + slot_rank
    left_tiles = jnp.take(tile_blocks, local_source, axis=2)
    right_tiles = jnp.take(tile_blocks, local_target, axis=2)
    cross = block_cross(left_tiles, right_tiles, divisor)
    slot_table = (
        jnp.zeros((band_size * CAP, TILE, 2 * bin_count), jnp.bfloat16).at[slot_index].set(cross)
    )
    arrived = lax.all_to_all(
        slot_table.reshape(band_size, CAP, TILE, 2 * bin_count),
        "band",
        split_axis=0,
        concat_axis=0,
        tiled=True,
    )

    def block_table(block_number):
        return lag_table(block_number * bin_count, bin_count, band_size * bin_count)

    all_weights = jax.vmap(block_table)(lax.iota(jnp.int32, band_size))
    added = jnp.einsum("bfg,boag->ofa", all_weights, arrived, preferred_element_type=jnp.float32)
    return stacks + added[None]


def solution(mesh):
    in_specs = (
        P(None, None, "chan", "band"),
        P(),
        P("chan", None, None),
        P("chan", None, None),
        P("chan", "band", None, None),
    )
    out_specs = P("chan", "band", None, None)
    return jax.shard_map(body, mesh=mesh, in_specs=in_specs, out_specs=out_specs, check_vma=False)
```

profile of v0, /device:TPU:1, one launch (start us, length us, event | category | flops | bytes accessed | tf_op | source)
XLA Modules:
  0.0 108.2 jit_solution(5933072379219072634)
XLA Ops:
  0.0 0.0 copy-start
  0.0 0.8 dynamic-slice_convert_fusion
  0.8 0.1 broadcast_bitcast_fusion
  0.9 0.0 copy-start.2
  0.9 0.0 copy-start.3
  0.9 0.0 copy-start.4
  0.9 1.0 convert_element_type.43
  1.9 0.1 fusion.15
  2.1 0.0 copy-done
  2.1 0.1 multiply_convert_fusion.2
  2.2 3.9 %collective-permute-start = (bf16[2,2,896,8]{2,3,1,0:T(8,128)(2,1)S(1)}, bf16[2,2,896,8]{2,3,1,0:T(8,128)(2,1)S(1)}, u32[]{:S(2)}, u32[]{:S(2)}) collective-permute-start(bf16[2,2,896,8]{2,3,1,0:T(8,128)(2,1)S(1)} %get-tuple-element.12), channel_id=1, source_target_pairs={{0,1},{1,2},{2,3},{4,5},{5,6},{6,7},{8,9},{9,10},{10,11},{12,13},{... | collective-permute-start | bytes 172040 | tf_op jit(solution)/shard_map/ppermute | solution.py:24
  6.2 1.3 %collective-permute-start.1 = (bf16[2,2,896,8]{2,3,1,0:T(8,128)(2,1)S(1)}, bf16[2,2,896,8]{2,3,1,0:T(8,128)(2,1)S(1)}, u32[]{:S(2)}, u32[]{:S(2)}) collective-permute-start(bf16[2,2,896,8]{2,3,1,0:T(8,128)(2,1)S(1)} %get-tuple-element.13), channel_id=1, source_target_pairs={{1,0},{2,1},{3,2},{5,4},{6,5},{7,6},{9,8},{10,9},{11,10},{13,12},{... | collective-permute-start | bytes 172040 | tf_op jit(solution)/shard_map/ppermute | solution.py:25
  7.5 0.0 copy-done.2
  7.5 0.0 copy-done.3
  7.5 0.2 fusion.17
  7.7 0.3 fusion.8
  8.1 0.0 copy-done.4
  8.1 0.2 convert_reduce_fusion
  8.3 0.0 collective-permute-done
  8.3 2.8 %collective-permute-done.1 = bf16[2,2,896,8]{2,3,1,0:T(8,128)(2,1)S(1)} collective-permute-done((bf16[2,2,896,8]{2,3,1,0:T(8,128)(2,1)S(1)}, bf16[2,2,896,8]{2,3,1,0:T(8,128)(2,1)S(1)}, u32[]{:S(2)}, u32[]{:S(2)}) %collective-permute-start.1) | collective-permute-done | bytes 57376 | tf_op jit(solution)/shard_map/ppermute | solution.py:25
  11.1 0.9 gather_fusion
  12.0 0.9 gather_fusion.1
  12.9 0.7 select_bitcast_fusion
  13.6 0.6 fusion.10
  14.2 0.2 fusion.13
  14.4 1.1 %broadcast_in_dim.15 = bf16[256,128,16]{1,2,0:T(8,128)(2,1)} broadcast(bf16[]{:T(256)} %constant.12.clone.1), dimensions={} | broadcast | bytes 1048578 | tf_op jit(solution)/shard_map/broadcast_in_dim | solution.py:96
  15.5 12.4 %scatter_fusion = bf16[256,128,16]{1,2,0:T(8,128)(2,1)} fusion(bf16[256,128,16]{1,2,0:T(8,128)(2,1)} %broadcast_in_dim.15, s32[128]{0:T(128)S(1)} %fusion.22, bf16[128,128,16]{1,2,0:T(8,128)(2,1)S(1)} %fusion.13), kind=kCustom, calls=%fused_computation.2 | custom fusion | bytes 1573376 | tf_op jit(solution)/shard_map/scatter | solution.py:96
  28.0 0.0 copy-start.1
  28.0 21.3 %all-to-all-start = ((bf16[128,2,128,16]{2,3,1,0:T(8,128)(2,1)}), bf16[128,2,128,16]{2,3,1,0:T(8,128)(2,1)S(1)}, u32[]{:S(2)}, u32[]{:S(2)}) async-start(bf16[128,2,128,16]{2,3,1,0:T(8,128)(2,1)} %bitcast.10), calls=%async_computation | async-start | bytes 2097152 | tf_op jit(solution)/shard_map/all_to_all | solution.py:98
  49.3 0.0 copy-done.1
  49.3 1.0 copy.14
  50.3 0.1 iota_add_fusion
  50.4 9.2 %multiply_convert_fusion.1 = (bf16[128,512,8]{1,2,0:T(8,128)(2,1)S(1)}, bf16[128,512,8]{1,2,0:T(8,128)(2,1)S(1)}) fusion(s32[128,8]{1,0:T(8,128)S(1)} %iota_add_fusion, s32[512]{0:T(512)S(1)} %iota_add_fusion.1), kind=kLoop, calls=%fused_computation.16 | loop fusion | flops 9961472 | bytes 2103296 | tf_op jit(solution)/shard_map/convert
  59.6 44.1 %all-to-all-done = bf16[128,2,128,16]{2,3,1,0:T(8,128)(2,1)S(1)} async-done(((bf16[128,2,128,16]{2,3,1,0:T(8,128)(2,1)}), bf16[128,2,128,16]{2,3,1,0:T(8,128)(2,1)S(1)}, u32[]{:S(2)}, u32[]{:S(2)}) %all-to-all-start) | async-done | bytes 1048608 | tf_op jit(solution)/shard_map/all_to_all | solution.py:98
  103.6 2.6 %fusion.7 = f32[1,2,512,128]{2,3,1,0:T(8,128)} fusion(f32[1,2,512,128]{2,3,1,0:T(8,128)} %copy.14, bf16[128,2,128,16]{2,3,1,0:T(8,128)(2,1)S(1)} %all-to-all-done, bf16[128,512,8]{1,2,0:T(8,128)(2,1)S(1)} %get-tuple-element.15, bf16[128,512,8]{1,2,0:T(8,128)(2,1)S(1)} %get-tuple-element.14), kind=kOutput, calls=%fused_computation.22 | convolution fusion | flops 541196288 | bytes 4194304 | tf_op jit(solution)/shard_map/bfg,boag->ofa/dot_general | solution.py:110
  106.2 2.0 %copy.15 = f32[1,2,512,128]{3,2,1,0:T(8,128)} copy(f32[1,2,512,128]{2,3,1,0:T(8,128)} %fusion.7) | data formatting | bytes 1048576 | tf_op jit(solution)/shard_map/add | solution.py:111
  (12 shorter events, 0.2 us)
Async XLA Ops:
  0.0 2.1 %copy-start = (bf16[2,2,4096,8]{2,3,1,0:T(8,128)(2,1)S(1)}, bf16[2,2,4096,8]{2,3,1,0:T(8,128)(2,1)}, u32[]{:S(2)}) copy-start(bf16[2,2,4096,8]{2,3,1,0:T(8,128)(2,1)} %param.7) | copy-start | bytes 786436
  0.9 6.6 %copy-start.2 = (s32[1,128,2]{1,2,0:T(2,128)S(1)}, s32[1,128,2]{1,2,0:T(2,128)}, u32[]{:S(2)}) copy-start(s32[1,128,2]{1,2,0:T(2,128)} %param.9) | copy-start | bytes 3076
  0.9 6.6 %copy-start.3 = (s32[2,128]{1,0:T(2,128)S(1)}, s32[2,128]{1,0:T(2,128)}, u32[]{:S(2)}) copy-start(s32[2,128]{1,0:T(2,128)} %param.8) | copy-start | bytes 3076
  0.9 7.1 %copy-start.4 = (s32[1,128,1]{1,2,0:T(1,128)S(1)}, s32[1,128,1]{1,2,0:T(1,128)}, u32[]{:S(2)}) copy-start(s32[1,128,1]{1,2,0:T(1,128)} %param.10) | copy-start | bytes 1540
  2.2 6.1 %collective-permute-start = (bf16[2,2,896,8]{2,3,1,0:T(8,128)(2,1)S(1)}, bf16[2,2,896,8]{2,3,1,0:T(8,128)(2,1)S(1)}, u32[]{:S(2)}, u32[]{:S(2)}) collective-permute-start(bf16[2,2,896,8]{2,3,1,0:T(8,128)(2,1)S(1)} %get-tuple-element.12), channel_id=1, source_target_pairs={{0,1},{1,2},{2,3},{4,5},{5,6},{6,7},{8,9},{9,10},{10,11},{12,13},{... | collective-permute-start | bytes 172040 | tf_op jit(solution)/shard_map/ppermute | solution.py:24
  6.2 4.9 %collective-permute-start.1 = (bf16[2,2,896,8]{2,3,1,0:T(8,128)(2,1)S(1)}, bf16[2,2,896,8]{2,3,1,0:T(8,128)(2,1)S(1)}, u32[]{:S(2)}, u32[]{:S(2)}) collective-permute-start(bf16[2,2,896,8]{2,3,1,0:T(8,128)(2,1)S(1)} %get-tuple-element.13), channel_id=1, source_target_pairs={{1,0},{2,1},{3,2},{5,4},{6,5},{7,6},{9,8},{10,9},{11,10},{13,12},{... | collective-permute-start | bytes 172040 | tf_op jit(solution)/shard_map/ppermute | solution.py:25
  28.0 21.3 %copy-start.1 = (f32[1,2,512,128]{3,2,1,0:T(8,128)S(1)}, f32[1,2,512,128]{3,2,1,0:T(8,128)}, u32[]{:S(2)}) copy-start(f32[1,2,512,128]{3,2,1,0:T(8,128)} %param.11) | copy-start | bytes 1572868
  28.0 75.7 %all-to-all-start = ((bf16[128,2,128,16]{2,3,1,0:T(8,128)(2,1)}), bf16[128,2,128,16]{2,3,1,0:T(8,128)(2,1)S(1)}, u32[]{:S(2)}, u32[]{:S(2)}) async-start(bf16[128,2,128,16]{2,3,1,0:T(8,128)(2,1)} %bitcast.10), calls=%async_computation | async-start | bytes 2097152 | tf_op jit(solution)/shard_map/all_to_all | solution.py:98
where the time goes:
time: 110 us; the launch traced here: 108 us
  waiting for transfers between devices  46.9 us (43%)
  starting transfers between devices  26.5 us (24%)
  local copies, waits for them, and re-layouts  18.5 us (17%)
  other arithmetic  13 us (12%)
  matrix products  3.03 us (3%)
    all_to_all x1, waiting for transfers between devices, body(): lax.all_to_all(slot_table.reshape(band_size, CAP, TILE, 2 * bin_count), '...  44.1 us
    all_to_all x1, starting transfers between devices, body(): lax.all_to_all(slot_table.reshape(band_size, CAP, TILE, 2 * bin_count), '...  21.3 us
    scatter x1, local copies, waits for them, and re-layouts, body(): jnp.zeros((band_size * CAP, TILE, 2 * bin_count), jnp.bfloat16)  12.4 us
    another operation x1, other arithmetic  9.19 us
    ppermute x1, starting transfers between devices, padded(): before = lax.ppermute(last, axis, up)  3.95 us
    ppermute x1, waiting for transfers between devices, padded(): after = lax.ppermute(first, axis, down)  2.8 us
    dot_general x1, matrix products, body(): jnp.einsum('bfg,boag->ofa', all_weights, arrived, preferred_element_type=...  2.57 us
  transfers between devices with their start and end apart: 3, of which 2 were waited for; matrix products, arithmetic and copies ran while one was open for 10% of the time, Pallas kernels for 0%

commit v1 on v0

v1 whole, which is shorter than its diff:
```python
import math

import jax
import jax.numpy as jnp
import numpy as np
from jax import lax
from jax.experimental import pallas as pl
from jax.experimental.pallas import tpu as pltpu
from jax.sharding import PartitionSpec as P

TILE = 128
LAGS = 512
NF = 1024
NY, NZ = 4, 16
CHIPS = NY * NZ
QUARTERS = 4
TQ = 32
BINS = 8
FLOOR = 1e-05
BF = jnp.bfloat16
F32 = jnp.float32


def lag_table():
    tau = np.arange(LAGS) - LAGS // 2
    phase = np.mod(tau[:, None] * np.arange(NF)[None, :], NF)
    angles = phase.astype(np.float32) * np.float32(2.0 * math.pi / NF)
    amplitude = np.float32(1.0 / math.sqrt(NF))
    both = np.stack([np.cos(angles) * amplitude, -np.sin(angles) * amplitude])
    both = both.astype(np.float32).astype(jnp.bfloat16)
    both = both.reshape(2, LAGS, NY, NZ, 2, BINS)
    return both.transpose(2, 4, 1, 0, 3, 5).reshape(NY * 2, LAGS, 2 * NZ * BINS)


def place(tile, part):
    if tile < 8:
        return part * 8 + tile
    if tile < 24:
        return 32 + part * 16 + tile - 8
    return 96 + part * 8 + tile - 24


def send(src, dst, send_sem, recv_sem, where):
    pltpu.make_async_remote_copy(
        src_ref=src,
        dst_ref=dst,
        send_sem=send_sem,
        recv_sem=recv_sem,
        device_id=where,
        device_id_type=pl.DeviceIdType.MESH,
    ).start()


def wait_for(ref, sem):
    pltpu.make_async_copy(ref, ref, sem).wait()


def selection(quarter, core, fl_ref, pt_ref, ow_ref, s_mat):
    ii = lax.broadcasted_iota(jnp.int32, (TILE, TILE), 0)
    jj = lax.broadcasted_iota(jnp.int32, (TILE, TILE), 1)

    def row(values):
        return jnp.broadcast_to(values.astype(F32), (TILE, TILE))

    own = row(ow_ref[...])
    own_c = own.T
    rank = jnp.sum(jnp.where((own_c == own) & (jj < ii), 1.0, 0.0), axis=1, keepdims=True)
    holder = (2 * (jj % CHIPS) + core).astype(F32)
    order = (jj // CHIPS).astype(F32)
    chosen = jnp.where((own_c == holder) & (rank == order), 1.0, 0.0)
    a = jnp.sum(chosen * (row(pt_ref[0:1, :]).T + 1.0), axis=0, keepdims=True) - 1.0
    t = jnp.sum(chosen * (row(pt_ref[1:2, :]).T + 1.0), axis=0, keepdims=True) - 1.0
    tiles = ii.astype(F32)
    flags_a, flags_t = [], []
    for w in range(2):
        fc = row(fl_ref[w : w + 1, :]).T
        flags_a.append(jnp.sum(jnp.where(tiles == a, fc, 0.0), axis=0, keepdims=True))
        flags_t.append(jnp.sum(jnp.where(tiles == t, fc, 0.0), axis=0, keepdims=True))
    together = flags_a[0] * flags_t[0] + flags_a[1] * flags_t[1]
    share = jnp.where(together > 1.5, 0.5, 1.0)
    first = (quarter * TQ).astype(F32)
    a_here = a - first
    t_here = t - first
    low, mid = ii < 32, ii < 96
    part = jnp.where(low, ii // 8, jnp.where(mid, (ii - 32) // 16, (ii - 96) // 8))
    tile = jnp.where(low, ii % 8, jnp.where(mid, 8 + ii % 16, 24 + ii % 8)).astype(F32)
    edge_part = jnp.where(low, ii // 8, jnp.where(ii < 64, (ii - 32) // 8, -1))
    edge_tile = jnp.where(low, ii % 8 - 8, 32 + ii % 8).astype(F32)
    for p in range(4):
        w = p // 2
        left = pl.ds(p * TILE, TILE)
        right = pl.ds((4 + p) * TILE, TILE)
        here = part == p
        s_mat[0:TILE, left] = jnp.where(
            here & (tile == a_here), flags_a[w] * share, 0.0
        ).astype(BF)
        s_mat[0:TILE, right] = jnp.where(here & (tile == t_here), flags_t[w], 0.0).astype(BF)
        s_mat[TILE : 2 * TILE, left] = jnp.zeros((TILE, TILE), BF)
        s_mat[TILE : 2 * TILE, right] = jnp.where(
            (edge_part == p) & (edge_tile == t_here), flags_t[w], 0.0
        ).astype(BF)


def kernel(
    x_hbm, fl_hbm, pt_hbm, ow_hbm, w_hbm, out_ref,
    x_v, fl_v, pt_v, ow_v, w_v, a_f, b_f, b_h, r, hs, h, s_mat, acc, y_h, q_h,
    in_sems, w_sem, send1, recv1, sib_send, sib_recv, edge_send, edge_recv, send2, recv2,
):
    band = lax.axis_index("band")
    quarter = lax.axis_index("chan")
    chip, core = band // 2, band % 2
    y, z = chip // NZ, chip % NZ
    other = chip * 2 + 1 - core
    up = (quarter + 1) % QUARTERS
    down = (quarter + QUARTERS - 1) % QUARTERS

    loads = [
        pltpu.make_async_copy(x_hbm, x_v, in_sems.at[0]),
        pltpu.make_async_copy(fl_hbm, fl_v, in_sems.at[1]),
        pltpu.make_async_copy(pt_hbm, pt_v, in_sems.at[2]),
        pltpu.make_async_copy(ow_hbm, ow_v, in_sems.at[3]),
    ]
    for load in loads:
        load.start()
    load_w = pltpu.make_async_copy(w_hbm, w_v, w_sem)
    load_w.start()

    barrier = pltpu.get_barrier_semaphore()

    def greet(to_band, to_chan):
        pl.semaphore_signal(
            barrier, inc=1, device_id=(to_band, to_chan), device_id_type=pl.DeviceIdType.MESH
        )

    @pl.loop(1, CHIPS)
    def _(i):
        greet(((chip + i) % CHIPS) * 2 + core, quarter)

    greet(other, quarter)
    for beside in (up, down):
        greet(band, beside)
        greet(other, beside)

    for load in loads:
        load.wait()

    for tile in range(TQ):
        lanes = pl.ds(tile * TILE, TILE)
        for w in range(2):
            re = x_v[2 * w, :, lanes].astype(F32)
            im = x_v[2 * w + 1, :, lanes].astype(F32)
            energy = jnp.sum(re * re + im * im, axis=0, keepdims=True)
            scale = lax.rsqrt(energy * (1.0 / BINS) + FLOOR)
            a_f[pl.ds(8 * place(tile, 2 * w), 8), :] = re * scale
            a_f[pl.ds(8 * place(tile, 2 * w + 1), 8), :] = im * scale
    for i in range(BINS):
        b_f[pl.ds(i, TILE, stride=BINS), :] = a_f[pl.ds(i, TILE, stride=BINS), :].T
    b_h[...] = b_f[...].astype(BF).reshape(CHIPS, 16, TILE)

    pl.semaphore_wait(barrier, CHIPS - 1 + 5)

    def exchange(src, dst, send_sem, recv_sems):
        for t in (1, 2, 3, 0):
            row = (y + t) % NY

            @pl.loop(1 if t == 0 else 0, NZ)
            def _(i):
                g = row * NZ + (z + i) % NZ
                send(
                    src.at[g], dst.at[chip], send_sem, recv_sems.at[t],
                    (g * 2 + core, quarter),
                )

        pltpu.make_async_copy(src.at[chip], dst.at[chip], recv_sems.at[0]).start()

    exchange(b_h, r.at[0], send1, recv1)

    selection(quarter, core, fl_v, pt_v, ow_v, s_mat)
    acc[...] = jnp.zeros_like(acc)
    load_w.wait()

    block = lax.broadcasted_iota(jnp.int32, (64, TILE), 1) // 32

    def arrive(t):
        chips = pl.ds(((y + NY - t) % NY) * NZ, NZ)
        wait_for(r.at[0, chips], recv1.at[t])
        send(r.at[0, chips], r.at[1, chips], sib_send, sib_recv.at[t], (other, quarter))
        rows = r[0, chips].reshape(4, 64, TILE).astype(F32)
        high = rows[3]
        low = rows[0]
        for q in range(3):
            high = jnp.where(block == q, pltpu.roll(rows[q], (32 * q + 32) % TILE, 1), high)
        for q in range(1, 4):
            low = jnp.where(block == q, pltpu.roll(rows[q], 32 * q, 1), low)
        hs[t, 0] = high.astype(BF)
        hs[t, 1] = low.astype(BF)
        for d, beside in ((0, up), (1, down)):
            send(hs.at[t, d], h.at[t, 0, d], edge_send, edge_recv.at[t], (band, beside))
            send(hs.at[t, d], h.at[t, 1, d], edge_send, edge_recv.at[t], (other, beside))

    def compute(t):
        row = (y + NY - t) % NY
        chips = pl.ds(row * NZ, NZ)
        wait_for(h.at[t], edge_recv.at[t])
        wait_for(r.at[1, chips], sib_recv.at[t])
        total = None
        for o in range(2):
            from_low = h[t, o, 0].astype(F32)
            from_high = h[t, o, 1].astype(F32)
            edge = jnp.concatenate(
                [
                    jnp.where(
                        block == 0,
                        pltpu.roll(from_low, (TILE - 32 * q) % TILE, 1) if q else from_low,
                        pltpu.roll(from_high, (TILE + 32 - 32 * q) % TILE, 1)
                        if q != 1
                        else from_high,
                    )
                    for q in range(4)
                ],
                axis=0,
            ).astype(BF)
            rows = jnp.concatenate([r[o, chips].reshape(2 * TILE, TILE), edge], axis=1)
            g = jnp.dot(rows, s_mat[...], preferred_element_type=F32)
            left = [g[:, p * TILE : (p + 1) * TILE] for p in range(4)]
            right = [g[:, (4 + p) * TILE : (5 + p) * TILE] for p in range(4)]
            re = (left[0] * right[0] + left[1] * right[1]) + (
                left[2] * right[2] + left[3] * right[3]
            )
            im = (left[0] * right[1] - left[1] * right[0]) + (
                left[2] * right[3] - left[3] * right[2]
            )
            re = re.reshape(NZ, 2, BINS, TILE)
            im = im.reshape(NZ, 2, BINS, TILE)
            cross = jnp.concatenate(
                [
                    jnp.concatenate(
                        [v[:, k].reshape(TILE, TILE).astype(BF) for k in range(2)], axis=1
                    )
                    for v in (re, im)
                ],
                axis=0,
            )
            index = row * 2 + (core if o == 0 else 1 - core)
            part = jnp.dot(w_v[index], cross, preferred_element_type=F32)
            total = part if total is None else total + part
        acc[...] += total

    arrive(1)

    @pl.loop(2, 4)
    def _(t):
        arrive(t)
        compute(t - 1)

    arrive(0)
    compute(3)
    compute(0)

    for k in range(2):
        for c in range(4):
            turned = acc[c * TILE : (c + 1) * TILE, k * TILE : (k + 1) * TILE].T
            for s in range(2):
                b_f[pl.ds(k * 8 + s * 4 + c, CHIPS, stride=16), :] = turned[
                    s * CHIPS : (s + 1) * CHIPS
                ]
    y_h[...] = b_f[...].astype(BF).reshape(CHIPS, 16, TILE)
    exchange(y_h, q_h, send2, recv2)

    for t in (1, 2, 3, 0):
        row = (y + NY - t) % NY
        chips = pl.ds(row * NZ, NZ)
        wait_for(q_h.at[chips], recv2.at[t])
        a_f[pl.ds(row * 256, 256), :] = q_h[chips].astype(F32).reshape(256, TILE)
    for s in range(2):
        for c in range(4):
            out_ref[s, c * TILE : (c + 1) * TILE, :] = a_f[
                pl.ds(s * 4 + c, TILE, stride=BINS), :
            ].T

    most = pl.ds(0, CHIPS - 1)
    wait_for(b_h.at[most], send1)
    wait_for(y_h.at[most], send2)
    wait_for(r.at[0], sib_send)
    wait_for(h, edge_send)


def body(spectra, window_flags, pair_tiles, owners, stacks):
    x = jnp.transpose(spectra, (0, 1, 3, 2)).reshape(4, BINS, TQ * TILE)
    pairs = pair_tiles[0].T
    held = owners[0].T
    table = jnp.asarray(lag_table())
    dma = pltpu.SemaphoreType.DMA
    added = pl.pallas_call(
        kernel,
        out_shape=jax.ShapeDtypeStruct((2, LAGS, TILE), F32),
        in_specs=[pl.BlockSpec(memory_space=pltpu.HBM)] * 5,
        out_specs=pl.BlockSpec(memory_space=pltpu.VMEM),
        scratch_shapes=[
            pltpu.VMEM((4, BINS, TQ * TILE), BF),
            pltpu.VMEM((2, TILE), jnp.int32),
            pltpu.VMEM((2, TILE), jnp.int32),
            pltpu.VMEM((1, TILE), jnp.int32),
            pltpu.VMEM((NY * 2, LAGS, 256), BF),
            pltpu.VMEM((1024, TILE), F32),
            pltpu.VMEM((1024, TILE), F32),
            pltpu.VMEM((CHIPS, 16, TILE), BF),
            pltpu.VMEM((2, CHIPS, 16, TILE), BF),
            pltpu.VMEM((4, 2, 64, TILE), BF),
            pltpu.VMEM((4, 2, 2, 64, TILE), BF),
            pltpu.VMEM((256, 1024), BF),
            pltpu.VMEM((LAGS, 256), F32),
            pltpu.VMEM((CHIPS, 16, TILE), BF),
            pltpu.VMEM((CHIPS, 16, TILE), BF),
            dma((4,)),
            dma(()),
            dma(()),
            dma((4,)),
            dma(()),
            dma((4,)),
            dma(()),
            dma((4,)),
            dma(()),
            dma((4,)),
        ],
        compiler_params=pltpu.CompilerParams(
            collective_id=0, has_side_effects=True, vmem_limit_bytes=48 << 20
        ),
    )(x, window_flags, pairs, held, table)
    return stacks + added[None]


def solution(mesh):
    in_specs = (
        P(None, None, "chan", "band"),
        P(),
        P("chan", None, None),
        P("chan", None, None),
        P("chan", "band", None, None),
    )
    out_specs = P("chan", "band", None, None)
    return jax.shard_map(body, mesh=mesh, in_specs=in_specs, out_specs=out_specs, check_vma=False)
```

time: 110 us -> 62.7 us (0.57); the launches traced: 108 us -> 62.5 us
  Pallas kernels: 0 us -> 57 us
  waiting for transfers between devices: 46.9 us -> 0 us
  starting transfers between devices: 26.5 us -> 0 us
  local copies, waits for them, and re-layouts: 18.5 us -> 4.56 us
  other arithmetic: 13 us -> 0.85 us
  matrix products: 3.03 us -> 0 us
    pallas_call x0 -> x1, Pallas kernels: none -> 57 us  [body(): pl.pallas_call(kernel, out_shape=jax.ShapeDtypeStruct((2, LAGS, TILE), F3...]
    all_to_all x1 -> x0, waiting for transfers between devices: 44.1 us -> none  [body(): lax.all_to_all(slot_table.reshape(band_size, CAP, TILE, 2 * bin_count), '...]
    all_to_all x1 -> x0, starting transfers between devices: 21.3 us -> none  [body(): lax.all_to_all(slot_table.reshape(band_size, CAP, TILE, 2 * bin_count), '...]
    scatter x1 -> x0, local copies, waits for them, and re-layouts: 12.4 us -> none  [body(): jnp.zeros((band_size * CAP, TILE, 2 * bin_count), jnp.bfloat16)]
    another operation x1 -> x0, other arithmetic: 9.19 us -> none
    ppermute x2 -> x0, starting transfers between devices: 5.24 us -> none  [the longest x1 3.95 us: padded(): before = lax.ppermute(last, axis, up)]
    unnamed x13 -> x12, local copies, waits for them, and re-layouts: 1.12 us -> 4.56 us
    dot_general x3 -> x0, matrix products: 3.03 us -> none  [the longest x1 2.57 us: body(): jnp.einsum('bfg,boag->ofa', all_weights, arrived, preferred_element_type=...]
  transfers between devices with their start and end apart: 3 -> 0, of which waited for: 2 -> 0; matrix products, arithmetic and copies ran while one was open for 10% -> 0% of each run, Pallas kernels for 0% -> 0%
where the time goes in v1:
time: 62.7 us; the launch traced here: 62.5 us
  Pallas kernels  57 us (91%)
  local copies, waits for them, and re-layouts  4.56 us (7%)
  other arithmetic  0.85 us (1%)
    pallas_call x1, Pallas kernels, body(): pl.pallas_call(kernel, out_shape=jax.ShapeDtypeStruct((2, LAGS, TILE), F3...  57 us
    unnamed x12, local copies, waits for them, and re-layouts  4.56 us

profile of v1, /device:TPU:1, one launch (start us, length us, event | category | flops | bytes accessed | tf_op | source)
XLA Modules:
  0.0 62.5 jit_solution(11644777616777780182)
XLA Ops:
  0.0 0.0 copy-start
  0.0 1.6 %copy-done = bf16[8,512,256]{2,1,0:T(8,128)(2,1)S(1)} copy-done((bf16[8,512,256]{2,1,0:T(8,128)(2,1)S(1)}, bf16[8,512,256]{2,1,0:T(8,128)(2,1)}, u32[]{:S(2)}) %copy-start) | copy-done | bytes 2097176
  1.6 0.0 copy-start.1
  1.6 0.9 %copy-done.1 = bf16[2,2,4096,8]{2,3,1,0:T(8,128)(2,1)S(1)} copy-done((bf16[2,2,4096,8]{2,3,1,0:T(8,128)(2,1)S(1)}, bf16[2,2,4096,8]{2,3,1,0:T(8,128)(2,1)}, u32[]{:S(2)}) %copy-start.1) | copy-done | bytes 262168
  2.5 0.0 copy-start.2
  2.5 0.7 %copy-done.2 = s32[2,128]{1,0:T(2,128)S(1)} copy-done((s32[2,128]{1,0:T(2,128)S(1)}, s32[2,128]{1,0:T(2,128)}, u32[]{:S(2)}) %copy-start.2) | copy-done | bytes 1048
  3.2 0.0 copy-start.3
  3.2 0.7 %copy-done.3 = s32[1,128,2]{1,2,0:T(2,128)S(1)} copy-done((s32[1,128,2]{1,2,0:T(2,128)S(1)}, s32[1,128,2]{1,2,0:T(2,128)}, u32[]{:S(2)}) %copy-start.3) | copy-done | bytes 1048
  3.9 0.0 copy-start.4
  3.9 0.7 %copy-done.4 = s32[1,128,1]{1,2,0:T(1,128)S(1)} copy-done((s32[1,128,1]{1,2,0:T(1,128)S(1)}, s32[1,128,1]{1,2,0:T(1,128)}, u32[]{:S(2)}) %copy-start.4) | copy-done | bytes 536
  4.6 0.0 copy-start.5
  4.6 57.0 %shard_map.64 = f32[2,512,128]{2,1,0:T(8,128)S(1)} custom-call(bf16[4,8,4096]{2,1,0:T(8,128)(2,1)S(1)} %bitcast.9, s32[2,128]{1,0:T(2,128)S(1)} %copy-done.2, s32[2,128]{1,0:T(2,128)S(1)} %bitcast.10, s32[1,128]{1,0:T(1,128)S(1)} %bitcast.11, bf16[8,512,256]{2,1,0:T(8,128)(2,1)S(1)} %copy-done), custom_call_target="tpu_custom_call" | custom-call | tf_op jit(solution)/shard_map/pallas_call | solution.py:294
  61.6 0.0 copy-done.5
  61.6 0.8 %bitcast_add_fusion = f32[1,2,512,128]{3,2,1,0:T(8,128)} fusion(f32[1,2,512,128]{3,2,1,0:T(8,128)S(1)} %copy-done.5, f32[2,512,128]{2,1,0:T(8,128)S(1)} %shard_map.64), kind=kLoop, calls=%fused_computation | loop fusion | flops 131072 | bytes 1572864 | tf_op jit(solution)/shard_map/add | solution.py:330
Async XLA Ops:
  0.0 1.6 %copy-start = (bf16[8,512,256]{2,1,0:T(8,128)(2,1)S(1)}, bf16[8,512,256]{2,1,0:T(8,128)(2,1)}, u32[]{:S(2)}) copy-start(bf16[8,512,256]{2,1,0:T(8,128)(2,1)} %constant.2.clone.w_hbm) | copy-start | bytes 6291460
  1.6 0.9 %copy-start.1 = (bf16[2,2,4096,8]{2,3,1,0:T(8,128)(2,1)S(1)}, bf16[2,2,4096,8]{2,3,1,0:T(8,128)(2,1)}, u32[]{:S(2)}) copy-start(bf16[2,2,4096,8]{2,3,1,0:T(8,128)(2,1)} %param.6) | copy-start | bytes 786436
  2.5 0.7 %copy-start.2 = (s32[2,128]{1,0:T(2,128)S(1)}, s32[2,128]{1,0:T(2,128)}, u32[]{:S(2)}) copy-start(s32[2,128]{1,0:T(2,128)} %fl_hbm.1) | copy-start | bytes 3076
  3.2 0.7 %copy-start.3 = (s32[1,128,2]{1,2,0:T(2,128)S(1)}, s32[1,128,2]{1,2,0:T(2,128)}, u32[]{:S(2)}) copy-start(s32[1,128,2]{1,2,0:T(2,128)} %param.8) | copy-start | bytes 3076
  3.9 0.7 %copy-start.4 = (s32[1,128,1]{1,2,0:T(1,128)S(1)}, s32[1,128,1]{1,2,0:T(1,128)}, u32[]{:S(2)}) copy-start(s32[1,128,1]{1,2,0:T(1,128)} %param.9) | copy-start | bytes 1540
  4.6 57.0 %copy-start.5 = (f32[1,2,512,128]{3,2,1,0:T(8,128)S(1)}, f32[1,2,512,128]{3,2,1,0:T(8,128)}, u32[]{:S(2)}) copy-start(f32[1,2,512,128]{3,2,1,0:T(8,128)} %param.10) | copy-start | bytes 1572868

commit v2 on v1

--- a/solution.py
+++ b/solution.py
@@ -324,7 +324,7 @@
             dma((4,)),
         ],
         compiler_params=pltpu.CompilerParams(
-            collective_id=0, has_side_effects=True, vmem_limit_bytes=48 << 20
+            collective_id=0, has_side_effects=True, vmem_limit_bytes=56 << 20
         ),
     )(x, window_flags, pairs, held, table)
     return stacks + added[None]

time: 62.7 us -> 59.7 us (0.952)
  local copies, waits for them, and re-layouts: 4.56 us -> 0.01 us
  other arithmetic: 0.85 us -> 1.89 us
  Pallas kernels: 57 us -> 57.7 us
    unnamed x12 -> x2, local copies, waits for them, and re-layouts: 4.56 us -> 0.01 us
    add x1, other arithmetic: 0.85 us -> 1.89 us  [body(): return stacks + added[None]]
where the time goes in v2:
time: 59.7 us; the launch traced here: 59.6 us
  Pallas kernels  57.7 us (97%)
  other arithmetic  1.89 us (3%)
    pallas_call x1, Pallas kernels, body(): pl.pallas_call(kernel, out_shape=jax.ShapeDtypeStruct((2, LAGS, TILE), F3...  57.7 us
    add x1, other arithmetic, body(): return stacks + added[None]  1.89 us

profile of v2, /device:TPU:1, one launch (start us, length us, event | category | flops | bytes accessed | tf_op | source)
XLA Modules:
  0.0 59.6 jit_solution(7502220698808429778)
XLA Ops:
  0.0 0.0 copy-start
  0.0 57.7 %shard_map.64 = f32[2,512,128]{2,1,0:T(8,128)} custom-call(bf16[4,8,4096]{2,1,0:T(8,128)(2,1)} %bitcast.9, s32[2,128]{1,0:T(2,128)} %fl_hbm.1, s32[2,128]{1,0:T(2,128)} %bitcast.10, s32[1,128]{1,0:T(1,128)} %bitcast.11, bf16[8,512,256]{2,1,0:T(8,128)(2,1)} %constant.2.clone.w_hbm), custom_call_target="tpu_custom_call" | custom-call | tf_op jit(solution)/shard_map/pallas_call | solution.py:294
  57.7 0.0 copy-done
  57.7 1.9 %bitcast_add_fusion = f32[1,2,512,128]{3,2,1,0:T(8,128)} fusion(f32[1,2,512,128]{3,2,1,0:T(8,128)S(1)} %copy-done, f32[2,512,128]{2,1,0:T(8,128)} %shard_map.64), kind=kLoop, calls=%fused_computation | loop fusion | flops 131072 | bytes 1572864 | tf_op jit(solution)/shard_map/add | solution.py:330
Async XLA Ops:
  0.0 57.7 %copy-start = (f32[1,2,512,128]{3,2,1,0:T(8,128)S(1)}, f32[1,2,512,128]{3,2,1,0:T(8,128)}, u32[]{:S(2)}) copy-start(f32[1,2,512,128]{3,2,1,0:T(8,128)} %param.10) | copy-start | bytes 1572868

commit v3 on v2

--- a/solution.py
+++ b/solution.py
@@ -28,8 +28,8 @@
     amplitude = np.float32(1.0 / math.sqrt(NF))
     both = np.stack([np.cos(angles) * amplitude, -np.sin(angles) * amplitude])
     both = both.astype(np.float32).astype(jnp.bfloat16)
-    both = both.reshape(2, LAGS, NY, NZ, 2, BINS)
-    return both.transpose(2, 4, 1, 0, 3, 5).reshape(NY * 2, LAGS, 2 * NZ * BINS)
+    both = both.reshape(2, LAGS, NY, NZ * 2 * BINS)
+    return both.transpose(2, 1, 0, 3).reshape(NY, LAGS, 4 * NZ * BINS)
 
 
 def place(tile, part):
@@ -55,7 +55,7 @@
     pltpu.make_async_copy(ref, ref, sem).wait()
 
 
-def selection(quarter, core, fl_ref, pt_ref, ow_ref, s_mat):
+def selection(quarter, y, core, fl_ref, pt_ref, ow_ref, s_mat):
     ii = lax.broadcasted_iota(jnp.int32, (TILE, TILE), 0)
     jj = lax.broadcasted_iota(jnp.int32, (TILE, TILE), 1)
 
@@ -65,8 +65,9 @@
     own = row(ow_ref[...])
     own_c = own.T
     rank = jnp.sum(jnp.where((own_c == own) & (jj < ii), 1.0, 0.0), axis=1, keepdims=True)
-    holder = (2 * (jj % CHIPS) + core).astype(F32)
-    order = (jj // CHIPS).astype(F32)
+    owner_y = (y + core + 2 * ((jj % 32) // NZ)) % NY
+    holder = ((owner_y * NZ + jj % NZ) * 2 + jj // 64).astype(F32)
+    order = ((jj // 32) % 2).astype(F32)
     chosen = jnp.where((own_c == holder) & (rank == order), 1.0, 0.0)
     a = jnp.sum(chosen * (row(pt_ref[0:1, :]).T + 1.0), axis=0, keepdims=True) - 1.0
     t = jnp.sum(chosen * (row(pt_ref[1:2, :]).T + 1.0), axis=0, keepdims=True) - 1.0
@@ -103,16 +104,30 @@
 
 def kernel(
     x_hbm, fl_hbm, pt_hbm, ow_hbm, w_hbm, out_ref,
-    x_v, fl_v, pt_v, ow_v, w_v, a_f, b_f, b_h, r, hs, h, s_mat, acc, y_h, q_h,
-    in_sems, w_sem, send1, recv1, sib_send, sib_recv, edge_send, edge_recv, send2, recv2,
+    x_v, fl_v, pt_v, ow_v, w_v, a_f, b_f, b_k, x_in, m, r, hs, h, s_mat, acc, y_f, y_h, q_h, ps, pr,
+    in_sems, w_sem, pre_send, pre_recv, send1, recv1, sib_send, sib_recv, edge_send, edge_recv,
+    send2, recv2, post_send, post_recv,
 ):
     band = lax.axis_index("band")
     quarter = lax.axis_index("chan")
     chip, core = band // 2, band % 2
     y, z = chip // NZ, chip % NZ
     other = chip * 2 + 1 - core
-    up = (quarter + 1) % QUARTERS
-    down = (quarter + QUARTERS - 1) % QUARTERS
+    up, down = quarter + 1, quarter - 1
+    has_up, has_down = quarter < QUARTERS - 1, quarter > 0
+
+    barrier = pltpu.get_barrier_semaphore()
+
+    def greet(to_band, to_chan):
+        pl.semaphore_signal(
+            barrier, inc=1, device_id=(to_band, to_chan), device_id_type=pl.DeviceIdType.MESH
+        )
+
+    def row_of(who, j):
+        return (y + who + 2 * j) % NY
+
+    def step(i):
+        return jnp.where(i % 2 == 1, NZ // 2 - (i + 1) // 2, NZ // 2 + i // 2)
 
     loads = [
         pltpu.make_async_copy(x_hbm, x_v, in_sems.at[0]),
@@ -125,21 +140,22 @@
     load_w = pltpu.make_async_copy(w_hbm, w_v, w_sem)
     load_w.start()
 
-    barrier = pltpu.get_barrier_semaphore()
-
-    def greet(to_band, to_chan):
-        pl.semaphore_signal(
-            barrier, inc=1, device_id=(to_band, to_chan), device_id_type=pl.DeviceIdType.MESH
-        )
-
-    @pl.loop(1, CHIPS)
+    @pl.loop(0, NZ)
     def _(i):
-        greet(((chip + i) % CHIPS) * 2 + core, quarter)
+        for j in range(2):
+            g = row_of(core, j) * NZ + (z + step(i)) % NZ
+
+            @pl.when(g != chip)
+            def _():
+                greet(g * 2 + core, quarter)
 
     greet(other, quarter)
-    for beside in (up, down):
-        greet(band, beside)
-        greet(other, beside)
+    for there, beside in ((has_up, up), (has_down, down)):
+
+        @pl.when(there)
+        def _():
+            greet(band, beside)
+            greet(other, beside)
 
     for load in loads:
         load.wait()
@@ -155,37 +171,89 @@
             a_f[pl.ds(8 * place(tile, 2 * w + 1), 8), :] = im * scale
     for i in range(BINS):
         b_f[pl.ds(i, TILE, stride=BINS), :] = a_f[pl.ds(i, TILE, stride=BINS), :].T
-    b_h[...] = b_f[...].astype(BF).reshape(CHIPS, 16, TILE)
-
-    pl.semaphore_wait(barrier, CHIPS - 1 + 5)
-
-    def exchange(src, dst, send_sem, recv_sems):
-        for t in (1, 2, 3, 0):
-            row = (y + t) % NY
-
-            @pl.loop(1 if t == 0 else 0, NZ)
-            def _(i):
-                g = row * NZ + (z + i) % NZ
+    for b in range(2):
+        b_k[b] = (
+            b_f[...].reshape(CHIPS, 2, BINS, TILE)[:, b].reshape(NY, 8, 16, TILE).astype(BF)
+        )
+
+    pl.semaphore_wait(
+        barrier, 32 + core + 2 * has_up.astype(jnp.int32) + 2 * has_down.astype(jnp.int32)
+    )
+
+    for b in range(2):
+        for j in range(2):
+            send(
+                b_k.at[b, row_of(1 - core, j)], x_in.at[b, j], pre_send, pre_recv.at[b],
+                (other, quarter),
+            )
+
+    def merge(b):
+        wait_for(x_in.at[b], pre_recv.at[b])
+        for j in range(2):
+            rows = b_f[pl.ds(row_of(core, j) * 256, 256), :]
+            own = rows.reshape(NZ, 2, BINS, TILE)[:, b]
+            theirs = x_in[b, j].astype(F32).reshape(NZ, BINS, TILE)
+            low = jnp.where(core == 0, own, theirs)
+            high = jnp.where(core == 0, theirs, own)
+            both = jnp.stack([low, high], axis=1)
+            m[b, j] = both.reshape(NZ, 16, TILE).astype(BF)
+
+    def dispatch(src, dst, b, j, send_sem, recv_sem):
+        to_y = row_of(core, j)
+        there = (j + core) % 2
+
+        @pl.loop(0, NZ)
+        def _(i):
+            to_z = (z + step(i)) % NZ
+            g = to_y * NZ + to_z
+
+            @pl.when(g != chip)
+            def _():
                 send(
-                    src.at[g], dst.at[chip], send_sem, recv_sems.at[t],
+                    src.at[b, j, to_z], dst.at[2 * b + there, z], send_sem, recv_sem(there),
                     (g * 2 + core, quarter),
                 )
 
-        pltpu.make_async_copy(src.at[chip], dst.at[chip], recv_sems.at[0]).start()
-
-    exchange(b_h, r.at[0], send1, recv1)
-
-    selection(quarter, core, fl_v, pt_v, ow_v, s_mat)
+        if j == 0:
+
+            @pl.when(core == 0)
+            def _():
+                pltpu.make_async_copy(src.at[b, 0, z], dst.at[2 * b, z], recv_sem(0)).start()
+
+    def left(src, b, j, send_sem):
+        wait_for(src.at[b, j, pl.ds(0, NZ - 1)], send_sem)
+        if j == 0:
+
+            @pl.when(core == 1)
+            def _():
+                wait_for(src.at[b, j, 0], send_sem)
+
+        else:
+            wait_for(src.at[b, j, 0], send_sem)
+
+    merge(0)
+    for j in range(2):
+        dispatch(m, r.at[0], 0, j, send1.at[j], lambda there: recv1.at[there])
+    merge(1)
+    selection(quarter, y, core, fl_v, pt_v, ow_v, s_mat)
     acc[...] = jnp.zeros_like(acc)
+    for d, there in ((0, has_down), (1, has_up)):
+
+        @pl.when(jnp.logical_not(there))
+        def _():
+            h[:, d] = jnp.zeros((4, 2, 64, TILE), BF)
+
+    for j in range(2):
+        left(m, 0, j, send1.at[j])
+        dispatch(m, r.at[0], 1, j, send1.at[2 + j], lambda there: recv1.at[2 + there])
     load_w.wait()
 
     block = lax.broadcasted_iota(jnp.int32, (64, TILE), 1) // 32
 
     def arrive(t):
-        chips = pl.ds(((y + NY - t) % NY) * NZ, NZ)
-        wait_for(r.at[0, chips], recv1.at[t])
-        send(r.at[0, chips], r.at[1, chips], sib_send, sib_recv.at[t], (other, quarter))
-        rows = r[0, chips].reshape(4, 64, TILE).astype(F32)
+        wait_for(r.at[0, t], recv1.at[t])
+        send(r.at[0, t], r.at[1, t], sib_send, sib_recv.at[t], (other, quarter))
+        rows = r[0, t].reshape(4, 64, TILE).astype(F32)
         high = rows[3]
         low = rows[0]
         for q in range(3):
@@ -194,19 +262,25 @@
             low = jnp.where(block == q, pltpu.roll(rows[q], 32 * q, 1), low)
         hs[t, 0] = high.astype(BF)
         hs[t, 1] = low.astype(BF)
-        for d, beside in ((0, up), (1, down)):
-            send(hs.at[t, d], h.at[t, 0, d], edge_send, edge_recv.at[t], (band, beside))
-            send(hs.at[t, d], h.at[t, 1, d], edge_send, edge_recv.at[t], (other, beside))
+        for d, there, beside in ((0, has_up, up), (1, has_down, down)):
+
+            @pl.when(there)
+            def _():
+                send(hs.at[t, d], h.at[t, d, 0], edge_send.at[d], edge_recv.at[t, d], (band, beside))
+                send(hs.at[t, d], h.at[t, d, 1], edge_send.at[d], edge_recv.at[t, d], (other, beside))
 
     def compute(t):
-        row = (y + NY - t) % NY
-        chips = pl.ds(row * NZ, NZ)
-        wait_for(h.at[t], edge_recv.at[t])
-        wait_for(r.at[1, chips], sib_recv.at[t])
+        for d, there in ((0, has_down), (1, has_up)):
+
+            @pl.when(there)
+            def _():
+                wait_for(h.at[t, d], edge_recv.at[t, d])
+
+        wait_for(r.at[1, t], sib_recv.at[t])
         total = None
         for o in range(2):
-            from_low = h[t, o, 0].astype(F32)
-            from_high = h[t, o, 1].astype(F32)
+            from_low = h[t, 0, o].astype(F32)
+            from_high = h[t, 1, o].astype(F32)
             edge = jnp.concatenate(
                 [
                     jnp.where(
@@ -220,7 +294,7 @@
                 ],
                 axis=0,
             ).astype(BF)
-            rows = jnp.concatenate([r[o, chips].reshape(2 * TILE, TILE), edge], axis=1)
+            rows = jnp.concatenate([r[o, t].reshape(2 * TILE, TILE), edge], axis=1)
             g = jnp.dot(rows, s_mat[...], preferred_element_type=F32)
             left = [g[:, p * TILE : (p + 1) * TILE] for p in range(4)]
             right = [g[:, (4 + p) * TILE : (5 + p) * TILE] for p in range(4)]
@@ -230,59 +304,72 @@
             im = (left[0] * right[1] - left[1] * right[0]) + (
                 left[2] * right[3] - left[3] * right[2]
             )
-            re = re.reshape(NZ, 2, BINS, TILE)
-            im = im.reshape(NZ, 2, BINS, TILE)
-            cross = jnp.concatenate(
-                [
-                    jnp.concatenate(
-                        [v[:, k].reshape(TILE, TILE).astype(BF) for k in range(2)], axis=1
-                    )
-                    for v in (re, im)
-                ],
-                axis=0,
-            )
-            index = row * 2 + (core if o == 0 else 1 - core)
+            cross = jnp.concatenate([re, im], axis=0).astype(BF)
+            index = row_of(core if o == 0 else 1 - core, t % 2)
             part = jnp.dot(w_v[index], cross, preferred_element_type=F32)
             total = part if total is None else total + part
-        acc[...] += total
-
+        acc[t // 2] += total
+
+    def finish(b):
+        for c in range(4):
+            turned = acc[b, c * TILE : (c + 1) * TILE, :].T
+            for s in range(4):
+                y_f[pl.ds(s * 4 + c, 32, stride=16), :] = turned[s * 32 : (s + 1) * 32]
+        y_h[b] = y_f[...].astype(BF).reshape(2, NZ, 16, TILE)
+        for j in range(2):
+            dispatch(y_h, q_h, b, j, send2.at[b, j], lambda there: recv2.at[b])
+
+    def put(values, b, who):
+        for j in range(2):
+            first = row_of(who, j) * 256 + b * 8
+            for i in range(NZ):
+                a_f[pl.ds(pl.multiple_of(first + i * 16, 8), 8), :] = values[j, i]
+
+    def collect(b):
+        halves = pl.ds(2 * b, 2)
+        wait_for(q_h.at[halves], recv2.at[b])
+        got = q_h[halves].astype(F32).reshape(2, NZ, 2, 8, TILE)
+        theirs = jnp.where(core == 0, got[:, :, 1], got[:, :, 0])
+        ps[b] = theirs.reshape(2, 8, 16, TILE).astype(BF)
+        send(ps.at[b], pr.at[b], post_send, post_recv.at[b], (other, quarter))
+        put(jnp.where(core == 0, got[:, :, 0], got[:, :, 1]), b, core)
+
+    def join(b):
+        wait_for(pr.at[b], post_recv.at[b])
+        put(pr[b].astype(F32).reshape(2, NZ, 8, TILE), b, 1 - core)
+
+    arrive(0)
     arrive(1)
-
-    @pl.loop(2, 4)
-    def _(t):
-        arrive(t)
-        compute(t - 1)
-
-    arrive(0)
+    compute(0)
+    compute(1)
+    finish(0)
+    arrive(2)
+    arrive(3)
+    compute(2)
     compute(3)
-    compute(0)
-
-    for k in range(2):
-        for c in range(4):
-            turned = acc[c * TILE : (c + 1) * TILE, k * TILE : (k + 1) * TILE].T
-            for s in range(2):
-                b_f[pl.ds(k * 8 + s * 4 + c, CHIPS, stride=16), :] = turned[
-                    s * CHIPS : (s + 1) * CHIPS
-                ]
-    y_h[...] = b_f[...].astype(BF).reshape(CHIPS, 16, TILE)
-    exchange(y_h, q_h, send2, recv2)
-
-    for t in (1, 2, 3, 0):
-        row = (y + NY - t) % NY
-        chips = pl.ds(row * NZ, NZ)
-        wait_for(q_h.at[chips], recv2.at[t])
-        a_f[pl.ds(row * 256, 256), :] = q_h[chips].astype(F32).reshape(256, TILE)
+    finish(1)
+    collect(0)
+    join(0)
+    collect(1)
+    join(1)
     for s in range(2):
         for c in range(4):
             out_ref[s, c * TILE : (c + 1) * TILE, :] = a_f[
                 pl.ds(s * 4 + c, TILE, stride=BINS), :
             ].T
 
-    most = pl.ds(0, CHIPS - 1)
-    wait_for(b_h.at[most], send1)
-    wait_for(y_h.at[most], send2)
+    for j in range(2):
+        left(m, 1, j, send1.at[2 + j])
+        for b in range(2):
+            left(y_h, b, j, send2.at[b, j])
+    wait_for(x_in, pre_send)
     wait_for(r.at[0], sib_send)
-    wait_for(h, edge_send)
+    wait_for(ps, post_send)
+    for d, there in ((0, has_up), (1, has_down)):
+
+        @pl.when(there)
+        def _():
+            wait_for(h.at[:, d], edge_send.at[d])
 
 
 def body(spectra, window_flags, pair_tiles, owners, stacks):
@@ -301,27 +388,36 @@
             pltpu.VMEM((2, TILE), jnp.int32),
             pltpu.VMEM((2, TILE), jnp.int32),
             pltpu.VMEM((1, TILE), jnp.int32),
-            pltpu.VMEM((NY * 2, LAGS, 256), BF),
+            pltpu.VMEM((NY, LAGS, 512), BF),
             pltpu.VMEM((1024, TILE), F32),
             pltpu.VMEM((1024, TILE), F32),
-            pltpu.VMEM((CHIPS, 16, TILE), BF),
-            pltpu.VMEM((2, CHIPS, 16, TILE), BF),
+            pltpu.VMEM((2, NY, 8, 16, TILE), BF),
+            pltpu.VMEM((2, 2, 8, 16, TILE), BF),
+            pltpu.VMEM((2, 2, NZ, 16, TILE), BF),
+            pltpu.VMEM((2, 4, NZ, 16, TILE), BF),
             pltpu.VMEM((4, 2, 64, TILE), BF),
             pltpu.VMEM((4, 2, 2, 64, TILE), BF),
             pltpu.VMEM((256, 1024), BF),
-            pltpu.VMEM((LAGS, 256), F32),
-            pltpu.VMEM((CHIPS, 16, TILE), BF),
-            pltpu.VMEM((CHIPS, 16, TILE), BF),
+            pltpu.VMEM((2, LAGS, TILE), F32),
+            pltpu.VMEM((512, TILE), F32),
+            pltpu.VMEM((2, 2, NZ, 16, TILE), BF),
+            pltpu.VMEM((4, NZ, 16, TILE), BF),
+            pltpu.VMEM((2, 2, 8, 16, TILE), BF),
+            pltpu.VMEM((2, 2, 8, 16, TILE), BF),
             dma((4,)),
             dma(()),
             dma(()),
+            dma((2,)),
+            dma((4,)),
             dma((4,)),
             dma(()),
             dma((4,)),
+            dma((2,)),
+            dma((4, 2)),
+            dma((2, 2)),
+            dma((2,)),
             dma(()),
-            dma((4,)),
-            dma(()),
-            dma((4,)),
+            dma((2,)),
         ],
         compiler_params=pltpu.CompilerParams(
             collective_id=0, has_side_effects=True, vmem_limit_bytes=56 << 20

time: 59.7 us -> 58.6 us (0.982)
  Pallas kernels: 57.7 us -> 56.5 us
    pallas_call x1, Pallas kernels: 57.7 us -> 56.5 us  [body(): pl.pallas_call(kernel, out_shape=jax.ShapeDtypeStruct((2, LAGS, TILE), F3...]
where the time goes in v3:
time: 58.6 us; the launch traced here: 58.4 us
  Pallas kernels  56.5 us (96%)
  other arithmetic  1.89 us (3%)
    pallas_call x1, Pallas kernels, body(): pl.pallas_call(kernel, out_shape=jax.ShapeDtypeStruct((2, LAGS, TILE), F3...  56.5 us
    add x1, other arithmetic, body(): return stacks + added[None]  1.89 us

profile of v3, /device:TPU:1, one launch (start us, length us, event | category | flops | bytes accessed | tf_op | source)
XLA Modules:
  0.0 58.4 jit_solution(5252591327895094872)
XLA Ops:
  0.0 0.0 copy-start
  0.0 56.5 %shard_map.64 = f32[2,512,128]{2,1,0:T(8,128)} custom-call(bf16[4,8,4096]{2,1,0:T(8,128)(2,1)} %bitcast.9, s32[2,128]{1,0:T(2,128)} %fl_hbm.1, s32[2,128]{1,0:T(2,128)} %bitcast.10, s32[1,128]{1,0:T(1,128)} %bitcast.11, bf16[4,512,512]{2,1,0:T(8,128)(2,1)} %constant.2.clone.w_hbm), custom_call_target="tpu_custom_call" | custom-call | tf_op jit(solution)/shard_map/pallas_call | solution.py:381
  56.5 0.0 copy-done
  56.5 1.9 %bitcast_add_fusion = f32[1,2,512,128]{3,2,1,0:T(8,128)} fusion(f32[1,2,512,128]{3,2,1,0:T(8,128)S(1)} %copy-done, f32[2,512,128]{2,1,0:T(8,128)} %shard_map.64), kind=kLoop, calls=%fused_computation | loop fusion | flops 131072 | bytes 1572864 | tf_op jit(solution)/shard_map/add | solution.py:426
Async XLA Ops:
  0.0 56.5 %copy-start = (f32[1,2,512,128]{3,2,1,0:T(8,128)S(1)}, f32[1,2,512,128]{3,2,1,0:T(8,128)}, u32[]{:S(2)}) copy-start(f32[1,2,512,128]{3,2,1,0:T(8,128)} %param.10) | copy-start | bytes 1572868

commit v4 on v3

--- a/solution.py
+++ b/solution.py
@@ -317,26 +317,24 @@
                 y_f[pl.ds(s * 4 + c, 32, stride=16), :] = turned[s * 32 : (s + 1) * 32]
         y_h[b] = y_f[...].astype(BF).reshape(2, NZ, 16, TILE)
         for j in range(2):
-            dispatch(y_h, q_h, b, j, send2.at[b, j], lambda there: recv2.at[b])
-
-    def put(values, b, who):
-        for j in range(2):
-            first = row_of(who, j) * 256 + b * 8
-            for i in range(NZ):
-                a_f[pl.ds(pl.multiple_of(first + i * 16, 8), 8), :] = values[j, i]
-
-    def collect(b):
-        halves = pl.ds(2 * b, 2)
-        wait_for(q_h.at[halves], recv2.at[b])
-        got = q_h[halves].astype(F32).reshape(2, NZ, 2, 8, TILE)
-        theirs = jnp.where(core == 0, got[:, :, 1], got[:, :, 0])
-        ps[b] = theirs.reshape(2, 8, 16, TILE).astype(BF)
-        send(ps.at[b], pr.at[b], post_send, post_recv.at[b], (other, quarter))
-        put(jnp.where(core == 0, got[:, :, 0], got[:, :, 1]), b, core)
-
-    def join(b):
-        wait_for(pr.at[b], post_recv.at[b])
-        put(pr[b].astype(F32).reshape(2, NZ, 8, TILE), b, 1 - core)
+            dispatch(y_h, q_h, b, j, send2.at[b, j], lambda there: recv2.at[2 * b + there])
+
+    def put(values, t, who):
+        first = row_of(who, t % 2) * 256 + t // 2 * 8
+        for i in range(NZ):
+            a_f[pl.ds(pl.multiple_of(first + i * 16, 8), 8), :] = values[i]
+
+    def collect(t):
+        wait_for(q_h.at[t], recv2.at[t])
+        got = q_h[t].astype(F32).reshape(NZ, 2, 8, TILE)
+        theirs = jnp.where(core == 0, got[:, 1], got[:, 0])
+        ps[t] = theirs.reshape(8, 16, TILE).astype(BF)
+        send(ps.at[t], pr.at[t], post_send, post_recv.at[t], (other, quarter))
+        put(jnp.where(core == 0, got[:, 0], got[:, 1]), t, core)
+
+    def join(t):
+        wait_for(pr.at[t], post_recv.at[t])
+        put(pr[t].astype(F32).reshape(NZ, 8, TILE), t, 1 - core)
 
     arrive(0)
     arrive(1)
@@ -348,10 +346,11 @@
     compute(2)
     compute(3)
     finish(1)
-    collect(0)
-    join(0)
-    collect(1)
-    join(1)
+    for t in range(4):
+        collect(t)
+        if t >= 1:
+            join(t - 1)
+    join(3)
     for s in range(2):
         for c in range(4):
             out_ref[s, c * TILE : (c + 1) * TILE, :] = a_f[
@@ -402,8 +401,8 @@
             pltpu.VMEM((512, TILE), F32),
             pltpu.VMEM((2, 2, NZ, 16, TILE), BF),
             pltpu.VMEM((4, NZ, 16, TILE), BF),
-            pltpu.VMEM((2, 2, 8, 16, TILE), BF),
-            pltpu.VMEM((2, 2, 8, 16, TILE), BF),
+            pltpu.VMEM((4, 8, 16, TILE), BF),
+            pltpu.VMEM((4, 8, 16, TILE), BF),
             dma((4,)),
             dma(()),
             dma(()),
@@ -415,14 +414,19 @@
             dma((2,)),
             dma((4, 2)),
             dma((2, 2)),
-            dma((2,)),
+            dma((4,)),
             dma(()),
-            dma((2,)),
+            dma((4,)),
         ],
         compiler_params=pltpu.CompilerParams(
-            collective_id=0, has_side_effects=True, vmem_limit_bytes=56 << 20
+            collective_id=0, has_side_effects=True, vmem_limit_bytes=32 << 20
         ),
-    )(x, window_flags, pairs, held, table)
+    )(
+        *(
+            pltpu.with_memory_space_constraint(v, pltpu.HBM)
+            for v in (x, window_flags, pairs, held, table)
+        )
+    )
     return stacks + added[None]
 
 

time: 58.6 us -> 56.7 us (0.968)
  other arithmetic: 1.89 us -> 0.85 us
  Pallas kernels: 56.5 us -> 55.7 us
    add x1, other arithmetic: 1.89 us -> 0.85 us  [body(): return stacks + added[None]]
    pallas_call x1, Pallas kernels: 56.5 us -> 55.7 us  [body(): pl.pallas_call(kernel, out_shape=jax.ShapeDtypeStruct((2, LAGS, TILE), F3...]
where the time goes in v4:
time: 56.7 us; the launch traced here: 56.6 us
  Pallas kernels  55.7 us (98%)
  other arithmetic  0.85 us (1%)
    pallas_call x1, Pallas kernels, body(): pl.pallas_call(kernel, out_shape=jax.ShapeDtypeStruct((2, LAGS, TILE), F3...  55.7 us

profile of v4, /device:TPU:1, one launch (start us, length us, event | category | flops | bytes accessed | tf_op | source)
XLA Modules:
  0.0 56.6 jit_solution(5837053653921058457)
XLA Ops:
  0.0 0.0 copy-start
  0.0 55.7 %shard_map.64 = f32[2,512,128]{2,1,0:T(8,128)S(1)} custom-call(bf16[4,8,4096]{2,1,0:T(8,128)(2,1)} %bitcast.9, s32[2,128]{1,0:T(2,128)} %fl_hbm.1, s32[2,128]{1,0:T(2,128)} %bitcast.10, s32[1,128]{1,0:T(1,128)} %bitcast.11, bf16[4,512,512]{2,1,0:T(8,128)(2,1)} %constant.2.clone.w_hbm), custom_call_target="tpu_custom_call" | custom-call | tf_op jit(solution)/shard_map/pallas_call | solution.py:380
  55.7 0.0 copy-done
  55.7 0.8 %bitcast_add_fusion = f32[1,2,512,128]{3,2,1,0:T(8,128)} fusion(f32[1,2,512,128]{3,2,1,0:T(8,128)S(1)} %copy-done, f32[2,512,128]{2,1,0:T(8,128)S(1)} %shard_map.64), kind=kLoop, calls=%fused_computation | loop fusion | flops 131072 | bytes 1572864 | tf_op jit(solution)/shard_map/add | solution.py:430
Async XLA Ops:
  0.0 55.7 %copy-start = (f32[1,2,512,128]{3,2,1,0:T(8,128)S(1)}, f32[1,2,512,128]{3,2,1,0:T(8,128)}, u32[]{:S(2)}) copy-start(f32[1,2,512,128]{3,2,1,0:T(8,128)} %param.10) | copy-start | bytes 1572868

commit v5 on v4

--- a/solution.py
+++ b/solution.py
@@ -129,6 +129,15 @@
     def step(i):
         return jnp.where(i % 2 == 1, NZ // 2 - (i + 1) // 2, NZ // 2 + i // 2)
 
+    @pl.loop(0, NZ)
+    def _(i):
+        for j in range(2):
+            g = row_of(core, j) * NZ + (z + step(i)) % NZ
+
+            @pl.when(g != chip)
+            def _():
+                greet(g * 2 + core, quarter)
+
     loads = [
         pltpu.make_async_copy(x_hbm, x_v, in_sems.at[0]),
         pltpu.make_async_copy(fl_hbm, fl_v, in_sems.at[1]),
@@ -139,15 +148,6 @@
         load.start()
     load_w = pltpu.make_async_copy(w_hbm, w_v, w_sem)
     load_w.start()
-
-    @pl.loop(0, NZ)
-    def _(i):
-        for j in range(2):
-            g = row_of(core, j) * NZ + (z + step(i)) % NZ
-
-            @pl.when(g != chip)
-            def _():
-                greet(g * 2 + core, quarter)
 
     greet(other, quarter)
     for there, beside in ((has_up, up), (has_down, down)):
@@ -171,16 +171,18 @@
             a_f[pl.ds(8 * place(tile, 2 * w + 1), 8), :] = im * scale
     for i in range(BINS):
         b_f[pl.ds(i, TILE, stride=BINS), :] = a_f[pl.ds(i, TILE, stride=BINS), :].T
-    for b in range(2):
-        b_k[b] = (
-            b_f[...].reshape(CHIPS, 2, BINS, TILE)[:, b].reshape(NY, 8, 16, TILE).astype(BF)
-        )
-
+    def round_batch(b):
+        rows = b_f[...].reshape(CHIPS, 2, BINS, TILE)[:, b]
+        b_k[b] = rows.reshape(NY, 8, 16, TILE).astype(BF)
+
+    round_batch(0)
     pl.semaphore_wait(
         barrier, 32 + core + 2 * has_up.astype(jnp.int32) + 2 * has_down.astype(jnp.int32)
     )
 
     for b in range(2):
+        if b == 1:
+            round_batch(1)
         for j in range(2):
             send(
                 b_k.at[b, row_of(1 - core, j)], x_in.at[b, j], pre_send, pre_recv.at[b],
@@ -243,9 +245,8 @@
         def _():
             h[:, d] = jnp.zeros((4, 2, 64, TILE), BF)
 
-    for j in range(2):
-        left(m, 0, j, send1.at[j])
-        dispatch(m, r.at[0], 1, j, send1.at[2 + j], lambda there: recv1.at[2 + there])
+    left(m, 0, 0, send1.at[0])
+    dispatch(m, r.at[0], 1, 0, send1.at[2], lambda there: recv1.at[2 + there])
     load_w.wait()
 
     block = lax.broadcasted_iota(jnp.int32, (64, TILE), 1) // 32
@@ -337,6 +338,8 @@
         put(pr[t].astype(F32).reshape(NZ, 8, TILE), t, 1 - core)
 
     arrive(0)
+    left(m, 0, 1, send1.at[1])
+    dispatch(m, r.at[0], 1, 1, send1.at[3], lambda there: recv1.at[2 + there])
     arrive(1)
     compute(0)
     compute(1)

time: 56.7 us -> 56.2 us (level)
  no operation moved by 1% of the time
where the time goes in v5:
time: 56.2 us; the launch traced here: 56.1 us
  Pallas kernels  55.2 us (98%)
  other arithmetic  0.85 us (2%)
    pallas_call x1, Pallas kernels, body(): pl.pallas_call(kernel, out_shape=jax.ShapeDtypeStruct((2, LAGS, TILE), F3...  55.2 us

profile of v5, /device:TPU:1, one launch (start us, length us, event | category | flops | bytes accessed | tf_op | source)
XLA Modules:
  0.0 56.1 jit_solution(6982896042784722540)
XLA Ops:
  0.0 0.0 copy-start
  0.0 55.2 %shard_map.64 = f32[2,512,128]{2,1,0:T(8,128)S(1)} custom-call(bf16[4,8,4096]{2,1,0:T(8,128)(2,1)} %bitcast.9, s32[2,128]{1,0:T(2,128)} %fl_hbm.1, s32[2,128]{1,0:T(2,128)} %bitcast.10, s32[1,128]{1,0:T(1,128)} %bitcast.11, bf16[4,512,512]{2,1,0:T(8,128)(2,1)} %constant.2.clone.w_hbm), custom_call_target="tpu_custom_call" | custom-call | tf_op jit(solution)/shard_map/pallas_call | solution.py:383
  55.2 0.0 copy-done
  55.2 0.8 %bitcast_add_fusion = f32[1,2,512,128]{3,2,1,0:T(8,128)} fusion(f32[1,2,512,128]{3,2,1,0:T(8,128)S(1)} %copy-done, f32[2,512,128]{2,1,0:T(8,128)S(1)} %shard_map.64), kind=kLoop, calls=%fused_computation | loop fusion | flops 131072 | bytes 1572864 | tf_op jit(solution)/shard_map/add | solution.py:433
Async XLA Ops:
  0.0 55.2 %copy-start = (f32[1,2,512,128]{3,2,1,0:T(8,128)S(1)}, f32[1,2,512,128]{3,2,1,0:T(8,128)}, u32[]{:S(2)}) copy-start(f32[1,2,512,128]{3,2,1,0:T(8,128)} %param.10) | copy-start | bytes 1572868

commit v6 on v5

--- a/solution.py
+++ b/solution.py
@@ -263,23 +263,27 @@
             low = jnp.where(block == q, pltpu.roll(rows[q], 32 * q, 1), low)
         hs[t, 0] = high.astype(BF)
         hs[t, 1] = low.astype(BF)
-        for d, there, beside in ((0, has_up, up), (1, has_down, down)):
-
-            @pl.when(there)
-            def _():
-                send(hs.at[t, d], h.at[t, d, 0], edge_send.at[d], edge_recv.at[t, d], (band, beside))
-                send(hs.at[t, d], h.at[t, d, 1], edge_send.at[d], edge_recv.at[t, d], (other, beside))
-
-    def compute(t):
-        for d, there in ((0, has_down), (1, has_up)):
-
-            @pl.when(there)
-            def _():
-                wait_for(h.at[t, d], edge_recv.at[t, d])
-
-        wait_for(r.at[1, t], sib_recv.at[t])
+        for o, core_to in ((0, band), (1, other)):
+            for d, there, beside in ((0, has_up, up), (1, has_down, down)):
+
+                @pl.when(there)
+                def _():
+                    send(
+                        hs.at[t, d], h.at[t, d, o], edge_send.at[d], edge_recv.at[t, d, o],
+                        (core_to, beside),
+                    )
+
+    def compute(t, halves=(0, 1)):
         total = None
-        for o in range(2):
+        for o in halves:
+            if o == 1:
+                wait_for(r.at[1, t], sib_recv.at[t])
+            for d, there in ((0, has_down), (1, has_up)):
+
+                @pl.when(there)
+                def _():
+                    wait_for(h.at[t, d, o], edge_recv.at[t, d, o])
+
             from_low = h[t, 0, o].astype(F32)
             from_high = h[t, 1, o].astype(F32)
             edge = jnp.concatenate(
@@ -341,13 +345,15 @@
     left(m, 0, 1, send1.at[1])
     dispatch(m, r.at[0], 1, 1, send1.at[3], lambda there: recv1.at[2 + there])
     arrive(1)
-    compute(0)
-    compute(1)
+    for o in range(2):
+        compute(0, (o,))
+        compute(1, (o,))
     finish(0)
     arrive(2)
     arrive(3)
-    compute(2)
-    compute(3)
+    for o in range(2):
+        compute(2, (o,))
+        compute(3, (o,))
     finish(1)
     for t in range(4):
         collect(t)
@@ -415,7 +421,7 @@
             dma(()),
             dma((4,)),
             dma((2,)),
-            dma((4, 2)),
+            dma((4, 2, 2)),
             dma((2, 2)),
             dma((4,)),
             dma(()),

time: 56.2 us -> 55.5 us (0.988)
  Pallas kernels: 55.2 us -> 54.3 us
    pallas_call x1, Pallas kernels: 55.2 us -> 54.3 us  [body(): pl.pallas_call(kernel, out_shape=jax.ShapeDtypeStruct((2, LAGS, TILE), F3...]
where the time goes in v6:
time: 55.5 us; the launch traced here: 55.2 us
  Pallas kernels  54.3 us (98%)
  other arithmetic  0.85 us (2%)
    pallas_call x1, Pallas kernels, body(): pl.pallas_call(kernel, out_shape=jax.ShapeDtypeStruct((2, LAGS, TILE), F3...  54.3 us

profile of v6, /device:TPU:1, one launch (start us, length us, event | category | flops | bytes accessed | tf_op | source)
XLA Modules:
  0.0 55.2 jit_solution(14934994913283413542)
XLA Ops:
  0.0 0.0 copy-start
  0.0 54.3 %shard_map.64 = f32[2,512,128]{2,1,0:T(8,128)S(1)} custom-call(bf16[4,8,4096]{2,1,0:T(8,128)(2,1)} %bitcast.9, s32[2,128]{1,0:T(2,128)} %fl_hbm.1, s32[2,128]{1,0:T(2,128)} %bitcast.10, s32[1,128]{1,0:T(1,128)} %bitcast.11, bf16[4,512,512]{2,1,0:T(8,128)(2,1)} %constant.2.clone.w_hbm), custom_call_target="tpu_custom_call" | custom-call | tf_op jit(solution)/shard_map/pallas_call | solution.py:389
  54.3 0.0 copy-done
  54.4 0.8 %bitcast_add_fusion = f32[1,2,512,128]{3,2,1,0:T(8,128)} fusion(f32[1,2,512,128]{3,2,1,0:T(8,128)S(1)} %copy-done, f32[2,512,128]{2,1,0:T(8,128)S(1)} %shard_map.64), kind=kLoop, calls=%fused_computation | loop fusion | flops 131072 | bytes 1572864 | tf_op jit(solution)/shard_map/add | solution.py:439
Async XLA Ops:
  0.0 54.3 %copy-start = (f32[1,2,512,128]{3,2,1,0:T(8,128)S(1)}, f32[1,2,512,128]{3,2,1,0:T(8,128)}, u32[]{:S(2)}) copy-start(f32[1,2,512,128]{3,2,1,0:T(8,128)} %param.10) | copy-start | bytes 1572868
